TPU v7x, 32 devices: a whole 2x2x4 slice. The times are simulated.
32 devices in a mesh: query: 8 (over z, x), head: 4 (over y, core).
Axes of the slice: x: 2, y: 2, z: 4, core: 2. Of those that a mesh axis runs over, the one named last changes fastest.
Arguments:
- queries: bfloat16 [8192, 4096], P('query', 'head'), may hold values from -12 to 12
- mem_keys: bfloat16 [512, 4096], P('head'), may hold values from -6 to 6
- mem_values: bfloat16 [512, 4096], P('head'), may hold values from -6 to 6
- grad_out: bfloat16 [8192, 4096], P('query', 'head'), may hold values from -3 to 3
Outputs:
- attended: bfloat16 [8192, 4096], P('query', 'head')
- query_gradients: bfloat16 [8192, 4096], P('query', 'head')
- grad_keys: bfloat16 [512, 4096], P(('query', 'head'))
- grad_values: bfloat16 [512, 4096], P(('query', 'head'))
All inputs are finite; a program needn't handle non-finite values.
Results may differ from a plain program's by a relative error of at most 0.025.
Values may be sent and summed in bfloat16 or wider, within the bound.
A program may use at most 64 MiB of HBM per device.

v0:
```python
import jax
import jax.numpy as jnp
from jax import lax
from jax.sharding import PartitionSpec as P

HEAD_DIM = 256


def per_device(queries, mem_keys, mem_values, grad_out):
    head_group = lax.axis_size("head")
    query_group = lax.axis_size("query")
    mem_rows, full_width = mem_keys.shape
    query_row_count, local_width = queries.shape
    local_heads = local_width // HEAD_DIM
    score_scale = HEAD_DIM ** (-0.5)
    split_keys = mem_keys.reshape(mem_rows, head_group, local_width)
    split_values = mem_values.reshape(mem_rows, head_group, local_width)
    local_key_block, local_value_block = (
        lax.all_to_all(split_keys, "head", split_axis=1, concat_axis=0, tiled=True),
        lax.all_to_all(split_values, "head", split_axis=1, concat_axis=0, tiled=True),
    )
    total_memory = mem_rows * head_group
    local_key_block = local_key_block.reshape(total_memory, local_heads, HEAD_DIM)
    local_value_block = local_value_block.reshape(total_memory, local_heads, HEAD_DIM)
    block_rows = 512
    block_count = query_row_count // block_rows
    query_blocks = queries.reshape(block_count, block_rows, local_heads, HEAD_DIM)
    cotan_blocks = grad_out.reshape(block_count, block_rows, local_heads, HEAD_DIM)

    def step(totals, pieces):
        key_total, value_total = totals
        query_tile, output_gradient_block = pieces
        scores = (
            jnp.einsum(
                "jlv,elv->lje", query_tile, local_key_block, preferred_element_type=jnp.float32
            )
            * score_scale
        )
        row_top = jnp.max(scores, axis=-1, keepdims=True)
        weights = jnp.exp(scores - row_top)
        attention_probabilities = (weights / jnp.sum(weights, axis=-1, keepdims=True)).astype(
            jnp.bfloat16
        )
        attended = jnp.einsum(
            "ijt,tia->jia",
            attention_probabilities,
            local_value_block,
            preferred_element_type=jnp.float32,
        ).astype(jnp.bfloat16)
        dprobs = jnp.einsum(
            "jlv,elv->lje",
            output_gradient_block,
            local_value_block,
            preferred_element_type=jnp.float32,
        )
        row_delta = jnp.sum(
            attention_probabilities.astype(jnp.float32) * dprobs, axis=-1, keepdims=True
        )
        score_gradients = (
            attention_probabilities.astype(jnp.float32) * (dprobs - row_delta) * score_scale
        ).astype(jnp.bfloat16)
        grad_query = jnp.einsum(
            "ijt,tia->jia", score_gradients, local_key_block, preferred_element_type=jnp.float32
        ).astype(jnp.bfloat16)
        key_total = key_total + jnp.einsum(
            "gqv,qgw->vgw", score_gradients, query_tile, preferred_element_type=jnp.float32
        )
        value_total = value_total + jnp.einsum(
            "gqv,qgw->vgw",
            attention_probabilities,
            output_gradient_block,
            preferred_element_type=jnp.float32,
        )
        return ((key_total, value_total), (attended, grad_query))

    empty = jnp.zeros((total_memory, local_heads, HEAD_DIM), jnp.float32)
    (key_total, value_total), (attended, query_gradients) = lax.scan(
        step, (empty, empty), (query_blocks, cotan_blocks)
    )
    attended = attended.reshape(query_row_count, local_width)
    query_gradients = query_gradients.reshape(query_row_count, local_width)
    share_rows = total_memory // (query_group * head_group)
    key_parts = key_total.reshape(query_group, head_group, share_rows, local_width)
    value_parts = value_total.reshape(query_group, head_group, share_rows, local_width)
    key_moved, value_moved = (
        lax.all_to_all(
            key_parts.astype(jnp.bfloat16), "head", split_axis=1, concat_axis=3, tiled=True
        ).astype(key_parts.dtype),
        lax.all_to_all(
            value_parts.astype(jnp.bfloat16), "head", split_axis=1, concat_axis=3, tiled=True
        ).astype(value_parts.dtype),
    )
    key_sum, value_sum = (
        lax.psum_scatter(
            key_moved.astype(jnp.bfloat16), "query", scatter_dimension=0, tiled=True
        ).astype(jnp.float32),
        lax.psum_scatter(
            value_moved.astype(jnp.bfloat16), "query", scatter_dimension=0, tiled=True
        ).astype(jnp.float32),
    )
    grad_keys = key_sum.astype(jnp.bfloat16)
    grad_values = value_sum.astype(jnp.bfloat16)
    grad_keys = grad_keys.reshape(share_rows, full_width)
    grad_values = grad_values.reshape(share_rows, full_width)
    return (attended, query_gradients, grad_keys, grad_values)


def solution(mesh):
    in_specs = (P("query", "head"), P("head", None), P("head", None), P("query", "head"))
    out_specs = (
        P("query", "head"),
        P("query", "head"),
        P(("query", "head"), None),
        P(("query", "head"), None),
    )
    return jax.shard_map(
        per_device, mesh=mesh, in_specs=in_specs, out_specs=out_specs, check_vma=False
    )
```

profile of v0, /device:TPU:0, one launch (start us, length us, event | category | flops | bytes accessed | tf_op | source)
XLA Modules:
  0.0 276.9 jit_solution(5078206876964904795)
XLA Ops:
  7.2 2.4 copy.101
  9.5 4.2 %all-to-all-start = ((bf16[128,4,1024]{2,0,1:T(8,128)(2,1)}), bf16[128,4,1024]{2,0,1:T(8,128)(2,1)S(1)}, u32[]{:S(2)}, u32[]{:S(2)}) async-start(bf16[128,4,1024]{2,0,1:T(8,128)(2,1)} %bitcast.65), calls=%async_computation | async-start | bytes 2097152 | tf_op jit(solution)/shard_map/all_to_all | solution.py:19
  13.8 1.1 copy.100
  14.9 13.4 %all-to-all-done = bf16[128,4,1024]{2,0,1:T(8,128)(2,1)S(1)} async-done(((bf16[128,4,1024]{2,0,1:T(8,128)(2,1)}), bf16[128,4,1024]{2,0,1:T(8,128)(2,1)S(1)}, u32[]{:S(2)}, u32[]{:S(2)}) %all-to-all-start) | async-done | bytes 1048608 | tf_op jit(solution)/shard_map/all_to_all | solution.py:19
  28.2 4.2 %all-to-all-start.1 = ((bf16[128,4,1024]{2,0,1:T(8,128)(2,1)}), bf16[128,4,1024]{2,0,1:T(8,128)(2,1)}, u32[]{:S(2)}, u32[]{:S(2)}) async-start(bf16[128,4,1024]{2,0,1:T(8,128)(2,1)} %bitcast.64), calls=%async_computation.1 | async-start | bytes 2097152 | tf_op jit(solution)/shard_map/all_to_all | solution.py:20
  32.6 3.3 %reshape.47 = bf16[2,512,4,256]{3,2,1,0:T(4,128)(2,1)S(1)} reshape(bf16[1024,1024]{1,0:T(8,128)(2,1)} %param.6) | data formatting | bytes 4194304 | tf_op jit(solution)/shard_map/reshape | solution.py:27
  35.9 4.5 %reshape.50 = bf16[2,512,4,256]{3,2,1,0:T(4,128)(2,1)} reshape(bf16[1024,1024]{1,0:T(8,128)(2,1)} %param.9) | data formatting | bytes 4194304 | tf_op jit(solution)/shard_map/reshape | solution.py:28
  40.4 1.6 reshape.49
  42.0 1.4 copy.61
  43.4 3.7 %all-to-all-done.1 = bf16[128,4,1024]{2,0,1:T(8,128)(2,1)} async-done(((bf16[128,4,1024]{2,0,1:T(8,128)(2,1)}), bf16[128,4,1024]{2,0,1:T(8,128)(2,1)}, u32[]{:S(2)}, u32[]{:S(2)}) %all-to-all-start.1) | async-done | bytes 1048608 | tf_op jit(solution)/shard_map/all_to_all | solution.py:20
  47.0 2.7 reshape.52
  49.7 2.4 copy.63
  52.1 65.3 %while.17 = (s32[]{:T(128)}, f32[512,4,256]{0,2,1:T(8,128)}, f32[512,4,256]{0,2,1:T(8,128)}, bf16[2,512,4,256]{3,2,1,0:T(4,128)(2,1)}, bf16[2,512,4,256]{3,2,1,0...) while((s32[]{:T(128)}, f32[512,4,256]{0,2,1:T(8,128)}, ...), condition=%wide.region_4.5_spmd.clone, body=%wide.region_0.4_spmd.clone.sunk | while | flops 3245348352 | bytes 134234608 | solution.py:77
  52.1 0.4 constant_dynamic-slice_fusion.4
  52.5 1.2 copy-done.2
  53.7 0.7 fusion.47
  54.5 2.7 fusion.48
  57.2 0.6 divide_convert_fusion.2
  57.9 1.0 copy-done.9
  58.8 0.4 constant_dynamic-slice_fusion.5
  59.2 2.7 fusion.49
  61.9 7.1 %bitcast_add_fusion.4 = f32[512,4,256]{0,2,1:T(8,128)} fusion(f32[512,4,256]{0,2,1:T(8,128)} %get-tuple-element.212, bf16[4,512,512]{1,2,0:T(8,128)(2,1)S(1)} %divide_convert_fusion.2, f32[4,512,512]{1,2,0:T(8,128)} %fusion.49, pred[]{:T(512)S(6)} %compare.3, bf16[1,512,4,256]{3,2,1,0:T(4,128)(2,1)} %copy-done.2), kind=kOutput, calls=%fused_computation.14.clone.1 | convolution fusion | flops 545262080 | bytes 11534337 | tf_op jit(solution)/shard_map/while/body/eval_jaxpr/gqv,qgw->vgw/dot_general | solution.py:65
  69.0 2.1 bitcast_add_fusion.5
  71.2 6.6 %fusion.50 = bf16[1,512,4,256]{3,1,2,0:T(8,128)(2,1)} fusion(bf16[512,4,256]{2,0,1:T(8,128)(2,1)} %copy-done.4, bf16[4,512,512]{1,2,0:T(8,128)(2,1)S(1)} %divide_convert_fusion.2, f32[4,512,512]{1,2,0:T(8,128)} %fusion.49), kind=kOutput, calls=%fused_computation.21.clone.1 | convolution fusion | flops 544737792 | bytes 8388608 | tf_op jit(solution)/shard_map/while/body/eval_jaxpr/ijt,tia->jia/dot_general | solution.py:62
  77.8 0.9 fusion.51
  78.7 0.3 copy-done.6
  79.0 0.7 copy-done.10
  79.7 2.6 copy_dynamic-update-slice_fusion.3
  82.3 1.4 copy-done.11
  83.7 0.4 constant_dynamic-slice_fusion.4
  84.1 1.2 copy-done.2
  85.3 0.7 fusion.47
  86.1 2.7 fusion.48
  88.8 0.6 divide_convert_fusion.2
  89.4 1.0 copy-done.9
  90.4 0.4 constant_dynamic-slice_fusion.5
  90.8 2.7 fusion.49
  93.5 7.7 %bitcast_add_fusion.4 = f32[512,4,256]{0,2,1:T(8,128)} fusion(f32[512,4,256]{0,2,1:T(8,128)} %get-tuple-element.212, bf16[4,512,512]{1,2,0:T(8,128)(2,1)S(1)} %divide_convert_fusion.2, f32[4,512,512]{1,2,0:T(8,128)} %fusion.49, pred[]{:T(512)S(6)} %compare.3, bf16[1,512,4,256]{3,2,1,0:T(4,128)(2,1)} %copy-done.2), kind=kOutput, calls=%fused_computation.14.clone.1 | convolution fusion | flops 545262080 | bytes 11534337 | tf_op jit(solution)/shard_map/while/body/eval_jaxpr/gqv,qgw->vgw/dot_general | solution.py:65
  101.2 3.7 %bitcast_add_fusion.5 = f32[512,4,256]{0,2,1:T(8,128)} fusion(f32[512,4,256]{0,2,1:T(8,128)} %get-tuple-element.213, bf16[4,512,512]{1,2,0:T(8,128)(2,1)S(1)} %divide_convert_fusion.2, pred[]{:T(512)S(6)} %compare.3, bf16[1,512,4,256]{3,2,1,0:T(4,128)(2,1)S(1)} %constant_dynamic-slice_fusion.5), kind=kOutput, calls=%fused_computation.13.clone.1 | convolution fusion | flops 537919488 | bytes 7340033 | tf_op jit(solution)/shard_map/while/body/eval_jaxpr/gqv,qgw->vgw/dot_general | solution.py:68
  104.9 6.6 %fusion.50 = bf16[1,512,4,256]{3,1,2,0:T(8,128)(2,1)} fusion(bf16[512,4,256]{2,0,1:T(8,128)(2,1)} %copy-done.4, bf16[4,512,512]{1,2,0:T(8,128)(2,1)S(1)} %divide_convert_fusion.2, f32[4,512,512]{1,2,0:T(8,128)} %fusion.49), kind=kOutput, calls=%fused_computation.21.clone.1 | convolution fusion | flops 544737792 | bytes 8388608 | tf_op jit(solution)/shard_map/while/body/eval_jaxpr/ijt,tia->jia/dot_general | solution.py:62
  111.6 0.9 fusion.51
  112.5 0.3 copy-done.6
  112.8 0.7 copy-done.10
  113.5 2.6 copy_dynamic-update-slice_fusion.3
  116.1 1.4 copy-done.11
  117.5 1.7 convert_element_type.42
  119.2 0.7 copy.66
  119.9 0.8 convert_element_type.43
  120.7 0.1 copy.67
  120.8 16.9 %all_to_all.66 = bf16[8,4,16,1024]{3,2,0,1:T(8,128)(2,1)S(1)} all-to-all(bf16[8,4,16,1024]{3,2,0,1:T(8,128)(2,1)S(1)} %copy.67), channel_id=1, replica_groups=mesh['query'=8,'head'=4] {'head'}, dimensions={1} | all-to-all | bytes 2097152 | tf_op jit(solution)/shard_map/all_to_all | solution.py:86
  137.7 1.1 copy.86
  138.8 0.8 copy-done.3
  139.6 0.1 convert_element_type.44
  139.8 0.7 copy.69
  140.5 0.8 convert_element_type.45
  141.3 0.1 copy.70
  141.4 16.9 %all_to_all.67 = bf16[8,4,16,1024]{3,2,0,1:T(8,128)(2,1)S(1)} all-to-all(bf16[8,4,16,1024]{3,2,0,1:T(8,128)(2,1)S(1)} %copy.70), channel_id=1, replica_groups=mesh['query'=8,'head'=4] {'head'}, dimensions={1} | all-to-all | bytes 2097152 | tf_op jit(solution)/shard_map/all_to_all | solution.py:89
  158.3 1.1 copy.87
  159.4 0.9 copy-done.12
  160.3 1.8 copy.88
  162.1 0.1 copy-done.13
  162.2 1.8 copy.89
  164.0 39.3 %reduce-scatter.3.cloned.1.call-done = bf16[1,1,16,4096]{3,2,0,1:T(8,128)(2,1)} async-done(((bf16[8,1,16,4096]{3,2,0,1:T(8,128)(2,1)}), bf16[1,1,16,4096]{3,2,0,1:T(8,128)(2,1)}) %reduce-scatter.3.cloned.1.call-update) | async-done | bytes 131088 | tf_op jit(solution)/shard_map/reduce_scatter | solution.py:94
  203.3 66.8 %reduce-scatter.5.cloned.1.call-done = bf16[1,1,16,4096]{3,2,0,1:T(8,128)(2,1)} async-done(((bf16[8,1,16,4096]{3,2,0,1:T(8,128)(2,1)}), bf16[1,1,16,4096]{3,2,0,1:T(8,128)(2,1)}) %reduce-scatter.5.cloned.1.call-update) | async-done | bytes 131088 | tf_op jit(solution)/shard_map/reduce_scatter | solution.py:97
  (47 shorter events, 0.3 us)
Async XLA Ops:
  7.2 6.6 %copy-start.14 = (bf16[128,4096]{1,0:T(8,128)(2,1)S(1)}, bf16[128,4096]{1,0:T(8,128)(2,1)}, u32[]{:S(2)}) copy-start(bf16[128,4096]{1,0:T(8,128)(2,1)} %param.8) | copy-start | bytes 3145732
  9.5 18.7 %all-to-all-start = ((bf16[128,4,1024]{2,0,1:T(8,128)(2,1)}), bf16[128,4,1024]{2,0,1:T(8,128)(2,1)S(1)}, u32[]{:S(2)}, u32[]{:S(2)}) async-start(bf16[128,4,1024]{2,0,1:T(8,128)(2,1)} %bitcast.65), calls=%async_computation | async-start | bytes 2097152 | tf_op jit(solution)/shard_map/all_to_all | solution.py:19
  28.2 18.8 %all-to-all-start.1 = ((bf16[128,4,1024]{2,0,1:T(8,128)(2,1)}), bf16[128,4,1024]{2,0,1:T(8,128)(2,1)}, u32[]{:S(2)}, u32[]{:S(2)}) async-start(bf16[128,4,1024]{2,0,1:T(8,128)(2,1)} %bitcast.64), calls=%async_computation.1 | async-start | bytes 2097152 | tf_op jit(solution)/shard_map/all_to_all | solution.py:20
  32.5 170.8 %reduce-scatter.3.cloned.1.call-start = ((), (), s32[]{:S(2)}) async-start(), calls=%async_computation.6 | async-start | bytes 1179648 | tf_op jit(solution)/shard_map/reduce_scatter | solution.py:94
  52.1 2.4 copy-start.4
  52.1 5.1 %copy-start.7 = (bf16[2,512,4,256]{3,2,1,0:T(4,128)(2,1)}, bf16[2,512,4,256]{3,2,1,0:T(4,128)(2,1)S(1)}, u32[]{:S(2)}) copy-start(bf16[2,512,4,256]{3,2,1,0:T(4,128)(2,1)S(1)} %get-tuple-element.227) | copy-start | bytes 6291460 | tf_op jit(solution)/shard_map/while
  52.5 1.2 copy-start.2
  57.2 1.6 copy-start.9
  57.8 1.4 copy-start
  71.2 6.6 %copy-start.1 = (bf16[512,4,256]{2,0,1:T(8,128)(2,1)S(1)}, bf16[512,4,256]{2,0,1:T(8,128)(2,1)}, u32[]{:S(2)}) copy-start(bf16[512,4,256]{2,0,1:T(8,128)(2,1)} %get-tuple-element.230) | copy-start | bytes 3145732 | tf_op jit(solution)/shard_map/while
  77.8 1.2 copy-start.6
  77.8 1.9 copy-start.10
  79.7 4.0 %copy-start.5 = (bf16[512,4,256]{2,0,1:T(8,128)(2,1)S(1)}, bf16[512,4,256]{2,0,1:T(8,128)(2,1)}, u32[]{:S(2)}) copy-start(bf16[512,4,256]{2,0,1:T(8,128)(2,1)} %copy-done.4) | copy-start | bytes 3145732 | tf_op jit(solution)/shard_map/while
  79.7 4.0 %copy-start.8 = (bf16[2,512,4,256]{3,2,1,0:T(4,128)(2,1)S(1)}, bf16[2,512,4,256]{3,2,1,0:T(4,128)(2,1)}, u32[]{:S(2)}) copy-start(bf16[2,512,4,256]{3,2,1,0:T(4,128)(2,1)} %copy-done.7) | copy-start | bytes 6291460 | tf_op jit(solution)/shard_map/while
  82.3 1.4 copy-start.11
  83.7 2.4 copy-start.4
  83.7 5.1 %copy-start.7 = (bf16[2,512,4,256]{3,2,1,0:T(4,128)(2,1)}, bf16[2,512,4,256]{3,2,1,0:T(4,128)(2,1)S(1)}, u32[]{:S(2)}) copy-start(bf16[2,512,4,256]{3,2,1,0:T(4,128)(2,1)S(1)} %get-tuple-element.227) | copy-start | bytes 6291460 | tf_op jit(solution)/shard_map/while
  84.1 1.2 copy-start.2
  88.8 1.6 copy-start.9
  89.4 1.4 copy-start
  104.9 6.6 %copy-start.1 = (bf16[512,4,256]{2,0,1:T(8,128)(2,1)S(1)}, bf16[512,4,256]{2,0,1:T(8,128)(2,1)}, u32[]{:S(2)}) copy-start(bf16[512,4,256]{2,0,1:T(8,128)(2,1)} %get-tuple-element.230) | copy-start | bytes 3145732 | tf_op jit(solution)/shard_map/while
  111.5 1.2 copy-start.6
  111.5 1.9 copy-start.10
  113.5 4.0 %copy-start.5 = (bf16[512,4,256]{2,0,1:T(8,128)(2,1)S(1)}, bf16[512,4,256]{2,0,1:T(8,128)(2,1)}, u32[]{:S(2)}) copy-start(bf16[512,4,256]{2,0,1:T(8,128)(2,1)} %copy-done.4) | copy-start | bytes 3145732 | tf_op jit(solution)/shard_map/while
  113.5 4.0 %copy-start.8 = (bf16[2,512,4,256]{3,2,1,0:T(4,128)(2,1)S(1)}, bf16[2,512,4,256]{3,2,1,0:T(4,128)(2,1)}, u32[]{:S(2)}) copy-start(bf16[2,512,4,256]{3,2,1,0:T(4,128)(2,1)} %copy-done.7) | copy-start | bytes 6291460 | tf_op jit(solution)/shard_map/while
  116.1 1.4 copy-start.11
  137.7 2.0 copy-start.3
  138.8 131.3 %reduce-scatter.5.cloned.1.call-start = ((), (), s32[]{:S(2)}) async-start(), calls=%async_computation.7 | async-start | bytes 1179648 | tf_op jit(solution)/shard_map/reduce_scatter | solution.py:97
  158.3 2.0 copy-start.12
  160.3 1.9 copy-start.13
Sparse Core Ops, SparseCore 0:
  138.9 64.3 reduce-scatter.2
  207.6 62.4 reduce-scatter.4
where the time goes:
time: 278 us; the launch traced here: 277 us
  waiting for transfers between devices  123 us (44%)
  local copies, waits for them, and re-layouts  46.1 us (17%)
  matrix products  42.6 us (15%)
  blocking collectives  33.8 us (12%)
  between operations  14.2 us (5%)
  starting transfers between devices  8.57 us (3%)
  other arithmetic  8.48 us (3%)
    reduce_scatter x1, waiting for transfers between devices, per_device(): lax.psum_scatter(value_moved.astype(jnp.bfloat16), 'query', scatter_dimen...  66.8 us
    reduce_scatter x1, waiting for transfers between devices, per_device(): lax.psum_scatter(key_moved.astype(jnp.bfloat16), 'query', scatter_dimensi...  39.3 us
    all_to_all x1, blocking collectives, per_device(): lax.all_to_all(key_parts.astype(jnp.bfloat16), 'head', split_axis=1, conc...  16.9 us
    all_to_all x1, blocking collectives, per_device(): lax.all_to_all(value_parts.astype(jnp.bfloat16), 'head', split_axis=1, co...  16.9 us
    dot_general x2, matrix products, step(): jnp.einsum('gqv,qgw->vgw', score_gradients, query_tile, preferred_element...  14.8 us
    all_to_all x1, waiting for transfers between devices, per_device(): lax.all_to_all(split_keys, 'head', split_axis=1, concat_axis=0, tiled=True)  13.4 us
    dot_general x2, matrix products, step(): jnp.einsum('ijt,tia->jia', score_gradients, local_key_block, preferred_el...  13.2 us
    while x44, local copies, waits for them, and re-layouts  9.26 us
  transfers between devices with their start and end apart: 4, of which 4 were waited for; matrix products, arithmetic and copies ran while one was open for 7% of the time, Pallas kernels for 0%

commit v1 on v0

v1 whole, which is shorter than its diff:
```python
import functools
import math

import jax
import jax.numpy as jnp
from jax import lax
from jax.experimental import pallas as pl
from jax.experimental.pallas import tpu as pltpu
from jax.sharding import PartitionSpec as P

HEAD_DIM = 256
MESH = pl.DeviceIdType.MESH
F32 = jnp.float32
BF16 = jnp.bfloat16
NT = (((1,), (1,)), ((), ()))


def kernel(
    sizes,
    q_hbm, k_hbm, v_hbm, o_hbm,
    att_hbm, dq_hbm, gk_ref, gv_ref,
    q_v, o_v, k_v, v_v, kt_v, vt_v, p_v, ds_v, att_v, dq_v,
    part, keep, x_in, z_out, z_in, h_out,
    kv_send, kv_recv, kv_own, qo_sem, out_sem,
    x_send, x_recv, z_send, z_recv, h_send, h_recv,
):
    heads, head_group, outer, rows, mem_rows, share, block = sizes
    memory = mem_rows * head_group
    piece = head_group * share
    me_q, me_h = lax.axis_index("query"), lax.axis_index("head")
    me_hi, me_lo = me_q // 2, me_q % 2
    scale = HEAD_DIM ** -0.5

    def head_peer(step):
        return me_q, lax.rem(me_h + step, head_group)

    def pair_peer():
        return me_hi * 2 + 1 - me_lo, me_h

    def outer_peer(step):
        return lax.rem(me_hi + step, outer) * 2 + me_lo, me_h

    head_steps = [s for s in range(2, head_group)] + [1]

    def kv_copy(j, step, which):
        src, dst = ((k_hbm, k_v), (v_hbm, v_v))[which]
        peer = head_peer(step)
        cols = pl.ds(pl.multiple_of((peer[1] * heads + j) * HEAD_DIM, HEAD_DIM), HEAD_DIM)
        mine = pl.ds(pl.multiple_of(me_h * mem_rows, mem_rows), mem_rows)
        return pltpu.make_async_remote_copy(
            src_ref=src.at[:, cols],
            dst_ref=dst.at[j, mine, :],
            send_sem=kv_send.at[j, step - 1, which],
            recv_sem=kv_recv.at[j, step - 1, which],
            device_id=peer,
            device_id_type=MESH,
        )

    def kv_local(j, which):
        src, dst = ((k_hbm, k_v), (v_hbm, v_v))[which]
        cols = pl.ds(pl.multiple_of((me_h * heads + j) * HEAD_DIM, HEAD_DIM), HEAD_DIM)
        mine = pl.ds(pl.multiple_of(me_h * mem_rows, mem_rows), mem_rows)
        return pltpu.make_async_copy(src.at[:, cols], dst.at[j, mine, :], kv_own.at[j, which])

    def qo_copy(j, which):
        src, dst = ((q_hbm, q_v), (o_hbm, o_v))[which]
        cols = pl.ds(pl.multiple_of(j * HEAD_DIM, HEAD_DIM), HEAD_DIM)
        return pltpu.make_async_copy(src.at[:, cols], dst.at[j], qo_sem.at[j, which])

    def out_copy(j, which):
        src, dst = ((att_v, att_hbm), (dq_v, dq_hbm))[which]
        cols = pl.ds(pl.multiple_of(j * HEAD_DIM, HEAD_DIM), HEAD_DIM)
        return pltpu.make_async_copy(src.at[j], dst.at[:, cols], out_sem.at[j, which])

    def x_copy(j, which):
        return pltpu.make_async_remote_copy(
            src_ref=part.at[j, which],
            dst_ref=x_in.at[j, which],
            send_sem=x_send.at[j, which],
            recv_sem=x_recv.at[j, which],
            device_id=pair_peer(),
            device_id_type=MESH,
        )

    def z_copy(j, step):
        return pltpu.make_async_remote_copy(
            src_ref=z_out.at[j, step - 1],
            dst_ref=z_in.at[j, step - 1],
            send_sem=z_send.at[j, step - 1],
            recv_sem=z_recv.at[j, step - 1],
            device_id=outer_peer(step),
            device_id_type=MESH,
        )

    def h_copy(j, step, which):
        peer = head_peer(step)
        cols = pl.ds(pl.multiple_of((me_h * heads + j) * HEAD_DIM, HEAD_DIM), HEAD_DIM)
        return pltpu.make_async_remote_copy(
            src_ref=h_out.at[j, which, peer[1]],
            dst_ref=(gk_ref, gv_ref)[which].at[:, cols],
            send_sem=h_send.at[j, step - 1, which],
            recv_sem=h_recv.at[j, step - 1, which],
            device_id=peer,
            device_id_type=MESH,
        )

    barrier = pltpu.get_barrier_semaphore()
    peers = [head_peer(s) for s in range(1, head_group)]
    peers += [pair_peer()] + [outer_peer(s) for s in range(1, outer)]
    for peer in peers:
        pl.semaphore_signal(barrier, inc=1, device_id=peer, device_id_type=MESH)
    for which in range(2):
        kv_local(0, which).start()
        qo_copy(0, which).start()
    pl.semaphore_wait(barrier, len(peers))

    def start_inputs(j, carry):
        for step in head_steps:
            for which in range(2):
                kv_copy(j, step, which).start()

        @pl.when(j > 0)
        def _():
            for which in range(2):
                kv_local(j, which).start()
                qo_copy(j, which).start()

        return carry

    lax.fori_loop(0, heads, start_inputs, 0)

    def rows_of(hi, lo):
        return pl.ds(pl.multiple_of((hi * 2 + lo) * piece, piece), piece)

    def work(j):
        for which in range(2):
            kv_local(j, which).wait()
            qo_copy(j, which).wait()
            for step in head_steps:
                kv_copy(j, step, which).wait_recv()
        kt_v[...] = k_v[j].T
        vt_v[...] = v_v[j].T

        def rows_block(r, carry):
            at = pl.ds(pl.multiple_of(r * block, block), block)
            scores = lax.dot_general(k_v[j], q_v[j, at, :], NT, preferred_element_type=F32)
            top = jnp.max(scores, axis=0, keepdims=True)
            weights = jnp.exp2((scores - top) * (scale * math.log2(math.e)))
            probs = (weights * (1.0 / jnp.sum(weights, axis=0, keepdims=True))).astype(BF16)
            p_v[:, at] = probs
            dprobs = lax.dot_general(v_v[j], o_v[j, at, :], NT, preferred_element_type=F32)
            probs32 = probs.astype(F32)
            delta = jnp.sum(probs32 * dprobs, axis=0, keepdims=True)
            dscores = (probs32 * (dprobs - delta)).astype(BF16)
            ds_v[:, at] = dscores
            att = jnp.dot(vt_v[...], probs, preferred_element_type=F32).astype(BF16)
            att_v[j, at, :] = att.T
            dq = (jnp.dot(kt_v[...], dscores, preferred_element_type=F32) * scale).astype(BF16)
            dq_v[j, at, :] = dq.T
            return carry

        lax.fori_loop(0, rows // block, rows_block, 0)
        for which in range(2):
            out_copy(j, which).start()

        for which in (1, 0):
            def piece_block(hi, carry):
                left = (ds_v, p_v)[which]
                right = (q_v, o_v)[which]
                for lo in range(2):
                    total = jnp.dot(
                        left[rows_of(hi, lo), :], right[j], preferred_element_type=F32
                    )
                    if which == 0:
                        total = total * scale

                    @pl.when(me_lo == lo)
                    def _():
                        keep[j, which, hi] = total

                    @pl.when(me_lo != lo)
                    def _():
                        part[j, which, hi] = total.astype(BF16)

                return carry

            lax.fori_loop(0, outer, piece_block, 0)
            x_copy(j, which).start()

    def pair_sum(j):
        for which in range(2):
            x_copy(j, which).wait()
            for step in range(1, outer):
                hi = lax.rem(me_hi + step, outer)
                total = keep[j, which, hi] + x_in[j, which, hi].astype(F32)
                z_out[j, step - 1, which] = total.astype(BF16)
            keep[j, which, me_hi] = keep[j, which, me_hi] + x_in[j, which, me_hi].astype(F32)
        for step in range(1, outer):
            z_copy(j, step).start()

    def outer_sum(j):
        for step in range(1, outer):
            z_copy(j, step).wait()
        for which in range(2):
            total = keep[j, which, me_hi]
            for step in range(1, outer):
                total = total + z_in[j, step - 1, which].astype(F32)
            for h in range(head_group):
                h_out[j, which, h] = total[h * share : (h + 1) * share].astype(BF16)
            for step in head_steps:
                h_copy(j, step, which).start()
            cols = pl.ds(pl.multiple_of((me_h * heads + j) * HEAD_DIM, HEAD_DIM), HEAD_DIM)
            (gk_ref, gv_ref)[which][:, cols] = h_out[j, which, me_h]

    def turn(t, carry):
        @pl.when(t < heads)
        def _():
            work(t)

        @pl.when(jnp.logical_and(t >= 1, t <= heads))
        def _():
            pair_sum(t - 1)

        @pl.when(t >= 2)
        def _():
            outer_sum(t - 2)

        return carry

    lax.fori_loop(0, heads + 2, turn, 0)

    def finish(j, carry):
        for which in range(2):
            out_copy(j, which).wait()
            for step in head_steps:
                kv_copy(j, step, which).wait_send()
                h_copy(j, step, which).wait()
        return carry

    lax.fori_loop(0, heads, finish, 0)


def per_device(queries, mem_keys, mem_values, grad_out):
    head_group = lax.axis_size("head")
    query_group = lax.axis_size("query")
    mem_rows, full_width = mem_keys.shape
    rows, local_width = queries.shape
    heads = local_width // HEAD_DIM
    memory = mem_rows * head_group
    outer = query_group // 2
    share = memory // (query_group * head_group)
    piece = head_group * share
    block = math.gcd(rows, 256)
    sizes = (heads, head_group, outer, rows, mem_rows, share, block)
    big = jax.ShapeDtypeStruct((rows, local_width), BF16)
    small = jax.ShapeDtypeStruct((share, full_width), BF16)
    flops = 12 * rows * memory * local_width
    anywhere = pl.BlockSpec(memory_space=pl.ANY)
    vmem = pl.BlockSpec(memory_space=pltpu.VMEM)
    dma = pltpu.SemaphoreType.DMA
    return tuple(pl.pallas_call(
        functools.partial(kernel, sizes),
        out_shape=(big, big, small, small),
        in_specs=[anywhere] * 4,
        out_specs=(anywhere, anywhere, vmem, vmem),
        scratch_shapes=[
            pltpu.VMEM((heads, rows, HEAD_DIM), BF16),
            pltpu.VMEM((heads, rows, HEAD_DIM), BF16),
            pltpu.VMEM((heads, memory, HEAD_DIM), BF16),
            pltpu.VMEM((heads, memory, HEAD_DIM), BF16),
            pltpu.VMEM((HEAD_DIM, memory), BF16),
            pltpu.VMEM((HEAD_DIM, memory), BF16),
            pltpu.VMEM((memory, rows), BF16),
            pltpu.VMEM((memory, rows), BF16),
            pltpu.VMEM((heads, rows, HEAD_DIM), BF16),
            pltpu.VMEM((heads, rows, HEAD_DIM), BF16),
            pltpu.VMEM((heads, 2, outer, piece, HEAD_DIM), BF16),
            pltpu.VMEM((heads, 2, outer, piece, HEAD_DIM), F32),
            pltpu.VMEM((heads, 2, outer, piece, HEAD_DIM), BF16),
            pltpu.VMEM((heads, outer - 1, 2, piece, HEAD_DIM), BF16),
            pltpu.VMEM((heads, outer - 1, 2, piece, HEAD_DIM), BF16),
            pltpu.VMEM((heads, 2, head_group, share, HEAD_DIM), BF16),
            dma((heads, head_group - 1, 2)),
            dma((heads, head_group - 1, 2)),
            dma((heads, 2)),
            dma((heads, 2)),
            dma((heads, 2)),
            dma((heads, 2)),
            dma((heads, 2)),
            dma((heads, outer - 1)),
            dma((heads, outer - 1)),
            dma((heads, head_group - 1, 2)),
            dma((heads, head_group - 1, 2)),
        ],
        compiler_params=pltpu.CompilerParams(
            collective_id=0, has_side_effects=True, vmem_limit_bytes=56 * 1024 * 1024
        ),
        cost_estimate=pl.CostEstimate(
            flops=flops,
            bytes_accessed=8 * rows * local_width + 4 * mem_rows * full_width,
            transcendentals=rows * memory * heads,
        ),
    )(queries, mem_keys, mem_values, grad_out))


def solution(mesh):
    in_specs = (P("query", "head"), P("head", None), P("head", None), P("query", "head"))
    out_specs = (
        P("query", "head"),
        P("query", "head"),
        P(("query", "head"), None),
        P(("query", "head"), None),
    )
    return jax.shard_map(
        per_device, mesh=mesh, in_specs=in_specs, out_specs=out_specs, check_vma=False
    )
```

time: 278 us -> 71.1 us (0.26)
  waiting for transfers between devices: 123 us -> 0 us
  Pallas kernels: 0 us -> 64.5 us
  matrix products: 42.6 us -> 0 us
  local copies, waits for them, and re-layouts: 46.1 us -> 5.87 us
  blocking collectives: 33.8 us -> 0 us
  between operations: 14.2 us -> 0.65 us
  starting transfers between devices: 8.57 us -> 0 us
  other arithmetic: 8.48 us -> 0 us
    reduce_scatter x2 -> x0, waiting for transfers between devices: 106 us -> none  [the longest x1 66.8 us: per_device(): lax.psum_scatter(value_moved.astype(jnp.bfloat16), 'query', scatter_dimen...]
    pallas_call x0 -> x1, Pallas kernels: none -> 64.5 us  [per_device(): pl.pallas_call(functools.partial(kernel, sizes), out_shape=(big, big, sma...]
    dot_general x12 -> x0, matrix products: 42.6 us -> none  [the longest x2 14.8 us: step(): jnp.einsum('gqv,qgw->vgw', score_gradients, query_tile, preferred_element...]
    all_to_all x2 -> x0, blocking collectives: 33.8 us -> none  [the longest x1 16.9 us: per_device(): lax.all_to_all(key_parts.astype(jnp.bfloat16), 'head', split_axis=1, conc...]
    all_to_all x2 -> x0, waiting for transfers between devices: 17 us -> none  [the longest x1 13.4 us: per_device(): lax.all_to_all(split_keys, 'head', split_axis=1, concat_axis=0, tiled=True)]
    reshape x6 -> x0, local copies, waits for them, and re-layouts: 15.6 us -> none  [the longest x1 4.51 us: per_device(): grad_out.reshape(block_count, block_rows, local_heads, HEAD_DIM)]
    while x44 -> x0, local copies, waits for them, and re-layouts: 9.26 us -> none
    all_to_all x2 -> x0, starting transfers between devices: 8.48 us -> none  [the longest x1 4.25 us: per_device(): lax.all_to_all(split_values, 'head', split_axis=1, concat_axis=0, tiled=T...]
  transfers between devices with their start and end apart: 4 -> 0, of which waited for: 4 -> 0; matrix products, arithmetic and copies ran while one was open for 7% -> 0% of each run, Pallas kernels for 0% -> 0%
where the time goes in v1:
time: 71.1 us; the launch traced here: 71 us
  Pallas kernels  64.5 us (91%)
  local copies, waits for them, and re-layouts  5.87 us (8%)
    pallas_call x1, Pallas kernels, per_device(): pl.pallas_call(functools.partial(kernel, sizes), out_shape=(big, big, sma...  64.5 us
    unnamed x10, local copies, waits for them, and re-layouts  5.87 us

profile of v1, /device:TPU:0, one launch (start us, length us, event | category | flops | bytes accessed | tf_op | source)
XLA Modules:
  0.0 71.0 jit_solution(2549297918971280287)
XLA Ops:
  0.6 64.5 %shard_map.75 = (bf16[1024,1024]{1,0:T(8,128)(2,1)}, bf16[1024,1024]{1,0:T(8,128)(2,1)}, bf16[16,4096]{1,0:T(8,128)(2,1)}, bf16[16,4096]{1,0:T(8,128)(2,1)}) custom-call(bf16[1024,1024]{1,0:T(8,128)(2,1)} %q_hbm.1, bf16[128,4096]{1,0:T(8,128)(2,1)} %k_hbm.1, bf16[128,4096]{1,0:T(8,128)(2,1)} %v_hbm.1, bf16[1024,1024]{1,0:T(8,128)(2,1)} %o_hbm.1), custom_call_target="tpu_custom_call" | custom-call | flops 6442450944 | bytes 10485760 | tf_op jit(solution)/shard_map/pallas_call | solution.py:261
  65.1 0.0 copy-start
  65.1 3.2 %copy.12 = bf16[1024,1024]{1,0:T(8,128)(2,1)} copy(bf16[1024,1024]{1,0:T(8,128)(2,1)} %get-tuple-element.8) | data formatting | bytes 4194304
  68.3 0.0 copy-done
  68.3 0.0 copy-start.2
  68.3 0.0 copy-start.1
  68.3 1.3 %copy.13 = bf16[1024,1024]{1,0:T(8,128)(2,1)} copy(bf16[1024,1024]{1,0:T(8,128)(2,1)S(1)} %copy-done) | data formatting | bytes 4194304
  69.7 0.0 copy-done.2
  69.7 0.7 copy.14
  70.3 0.0 copy-done.1
  70.3 0.7 copy.15
Async XLA Ops:
  65.1 3.2 %copy-start = (bf16[1024,1024]{1,0:T(8,128)(2,1)S(1)}, bf16[1024,1024]{1,0:T(8,128)(2,1)}, u32[]{:S(2)}) copy-start(bf16[1024,1024]{1,0:T(8,128)(2,1)} %get-tuple-element.9) | copy-start | bytes 6291460
  68.3 1.3 %copy-start.2 = (bf16[16,4096]{1,0:T(8,128)(2,1)S(1)}, bf16[16,4096]{1,0:T(8,128)(2,1)}, u32[]{:S(2)}) copy-start(bf16[16,4096]{1,0:T(8,128)(2,1)} %get-tuple-element.10) | copy-start | bytes 393220
  68.3 2.0 %copy-start.1 = (bf16[16,4096]{1,0:T(8,128)(2,1)S(1)}, bf16[16,4096]{1,0:T(8,128)(2,1)}, u32[]{:S(2)}) copy-start(bf16[16,4096]{1,0:T(8,128)(2,1)} %get-tuple-element.11) | copy-start | bytes 393220

commit v2 on v1

--- a/solution.py
+++ b/solution.py
@@ -129,9 +129,6 @@
 
     lax.fori_loop(0, heads, start_inputs, 0)
 
-    def rows_of(hi, lo):
-        return pl.ds(pl.multiple_of((hi * 2 + lo) * piece, piece), piece)
-
     def work(j):
         for which in range(2):
             kv_local(j, which).wait()
@@ -141,14 +138,23 @@
         kt_v[...] = k_v[j].T
         vt_v[...] = v_v[j].T
 
-        def rows_block(r, carry):
-            at = pl.ds(pl.multiple_of(r * block, block), block)
+        def products(r):
+            at = slice(r * block, (r + 1) * block)
             scores = lax.dot_general(k_v[j], q_v[j, at, :], NT, preferred_element_type=F32)
+            dprobs = lax.dot_general(v_v[j], o_v[j, at, :], NT, preferred_element_type=F32)
+            return scores, dprobs
+
+        blocks = rows // block
+        ahead = products(0)
+        for r in range(blocks):
+            scores, dprobs = ahead
+            if r + 1 < blocks:
+                ahead = products(r + 1)
+            at = slice(r * block, (r + 1) * block)
             top = jnp.max(scores, axis=0, keepdims=True)
             weights = jnp.exp2((scores - top) * (scale * math.log2(math.e)))
             probs = (weights * (1.0 / jnp.sum(weights, axis=0, keepdims=True))).astype(BF16)
             p_v[:, at] = probs
-            dprobs = lax.dot_general(v_v[j], o_v[j, at, :], NT, preferred_element_type=F32)
             probs32 = probs.astype(F32)
             delta = jnp.sum(probs32 * dprobs, axis=0, keepdims=True)
             dscores = (probs32 * (dprobs - delta)).astype(BF16)
@@ -157,34 +163,18 @@
             att_v[j, at, :] = att.T
             dq = (jnp.dot(kt_v[...], dscores, preferred_element_type=F32) * scale).astype(BF16)
             dq_v[j, at, :] = dq.T
-            return carry
-
-        lax.fori_loop(0, rows // block, rows_block, 0)
+
         for which in range(2):
             out_copy(j, which).start()
 
         for which in (1, 0):
-            def piece_block(hi, carry):
-                left = (ds_v, p_v)[which]
-                right = (q_v, o_v)[which]
-                for lo in range(2):
-                    total = jnp.dot(
-                        left[rows_of(hi, lo), :], right[j], preferred_element_type=F32
-                    )
-                    if which == 0:
-                        total = total * scale
-
-                    @pl.when(me_lo == lo)
-                    def _():
-                        keep[j, which, hi] = total
-
-                    @pl.when(me_lo != lo)
-                    def _():
-                        part[j, which, hi] = total.astype(BF16)
-
-                return carry
-
-            lax.fori_loop(0, outer, piece_block, 0)
+            left = (ds_v, p_v)[which]
+            right = (q_v, o_v)[which]
+            total = jnp.dot(left[...], right[j], preferred_element_type=F32)
+            if which == 0:
+                total = total * scale
+            keep[j, which] = total.reshape(outer, 2, piece, HEAD_DIM)
+            part[j, which] = keep[j, which, :, 1 - me_lo].astype(BF16)
             x_copy(j, which).start()
 
     def pair_sum(j):
@@ -192,9 +182,9 @@
             x_copy(j, which).wait()
             for step in range(1, outer):
                 hi = lax.rem(me_hi + step, outer)
-                total = keep[j, which, hi] + x_in[j, which, hi].astype(F32)
+                total = keep[j, which, hi, me_lo] + x_in[j, which, hi].astype(F32)
                 z_out[j, step - 1, which] = total.astype(BF16)
-            keep[j, which, me_hi] = keep[j, which, me_hi] + x_in[j, which, me_hi].astype(F32)
+            keep[j, which, me_hi, me_lo] += x_in[j, which, me_hi].astype(F32)
         for step in range(1, outer):
             z_copy(j, step).start()
 
@@ -202,7 +192,7 @@
         for step in range(1, outer):
             z_copy(j, step).wait()
         for which in range(2):
-            total = keep[j, which, me_hi]
+            total = keep[j, which, me_hi, me_lo]
             for step in range(1, outer):
                 total = total + z_in[j, step - 1, which].astype(F32)
             for h in range(head_group):
@@ -275,7 +265,7 @@
             pltpu.VMEM((heads, rows, HEAD_DIM), BF16),
             pltpu.VMEM((heads, rows, HEAD_DIM), BF16),
             pltpu.VMEM((heads, 2, outer, piece, HEAD_DIM), BF16),
-            pltpu.VMEM((heads, 2, outer, piece, HEAD_DIM), F32),
+            pltpu.VMEM((heads, 2, outer, 2, piece, HEAD_DIM), F32),
             pltpu.VMEM((heads, 2, outer, piece, HEAD_DIM), BF16),
             pltpu.VMEM((heads, outer - 1, 2, piece, HEAD_DIM), BF16),
             pltpu.VMEM((heads, outer - 1, 2, piece, HEAD_DIM), BF16),

time: 71.1 us -> 58.3 us (0.82)
  Pallas kernels: 64.5 us -> 51.7 us
    pallas_call x1, Pallas kernels: 64.5 us -> 51.7 us  [per_device(): pl.pallas_call(functools.partial(kernel, sizes), out_shape=(big, big, sma...]
where the time goes in v2:
time: 58.3 us; the launch traced here: 58.2 us
  Pallas kernels  51.7 us (89%)
  local copies, waits for them, and re-layouts  5.87 us (10%)
  between operations  0.65 us (1%)
    pallas_call x1, Pallas kernels, per_device(): pl.pallas_call(functools.partial(kernel, sizes), out_shape=(big, big, sma...  51.7 us
    unnamed x10, local copies, waits for them, and re-layouts  5.87 us

profile of v2, /device:TPU:0, one launch (start us, length us, event | category | flops | bytes accessed | tf_op | source)
XLA Modules:
  0.0 58.2 jit_solution(2043904787216408287)
XLA Ops:
  0.6 51.7 %shard_map.75 = (bf16[1024,1024]{1,0:T(8,128)(2,1)}, bf16[1024,1024]{1,0:T(8,128)(2,1)}, bf16[16,4096]{1,0:T(8,128)(2,1)}, bf16[16,4096]{1,0:T(8,128)(2,1)}) custom-call(bf16[1024,1024]{1,0:T(8,128)(2,1)} %q_hbm.1, bf16[128,4096]{1,0:T(8,128)(2,1)} %k_hbm.1, bf16[128,4096]{1,0:T(8,128)(2,1)} %v_hbm.1, bf16[1024,1024]{1,0:T(8,128)(2,1)} %o_hbm.1), custom_call_target="tpu_custom_call" | custom-call | flops 6442450944 | bytes 10485760 | tf_op jit(solution)/shard_map/pallas_call | solution.py:251
  52.3 0.0 copy-start
  52.3 3.2 %copy.12 = bf16[1024,1024]{1,0:T(8,128)(2,1)} copy(bf16[1024,1024]{1,0:T(8,128)(2,1)} %get-tuple-element.8) | data formatting | bytes 4194304
  55.5 0.0 copy-done
  55.5 0.0 copy-start.2
  55.5 0.0 copy-start.1
  55.5 1.3 %copy.13 = bf16[1024,1024]{1,0:T(8,128)(2,1)} copy(bf16[1024,1024]{1,0:T(8,128)(2,1)S(1)} %copy-done) | data formatting | bytes 4194304
  56.9 0.0 copy-done.2
  56.9 0.7 %copy.14 = bf16[16,4096]{1,0:T(8,128)(2,1)} copy(bf16[16,4096]{1,0:T(8,128)(2,1)S(1)} %copy-done.2) | data formatting | bytes 262144
  57.5 0.0 copy-done.1
  57.5 0.7 %copy.15 = bf16[16,4096]{1,0:T(8,128)(2,1)} copy(bf16[16,4096]{1,0:T(8,128)(2,1)S(1)} %copy-done.1) | data formatting | bytes 262144
Async XLA Ops:
  52.3 3.2 %copy-start = (bf16[1024,1024]{1,0:T(8,128)(2,1)S(1)}, bf16[1024,1024]{1,0:T(8,128)(2,1)}, u32[]{:S(2)}) copy-start(bf16[1024,1024]{1,0:T(8,128)(2,1)} %get-tuple-element.9) | copy-start | bytes 6291460
  55.5 1.3 %copy-start.2 = (bf16[16,4096]{1,0:T(8,128)(2,1)S(1)}, bf16[16,4096]{1,0:T(8,128)(2,1)}, u32[]{:S(2)}) copy-start(bf16[16,4096]{1,0:T(8,128)(2,1)} %get-tuple-element.10) | copy-start | bytes 393220
  55.5 2.0 %copy-start.1 = (bf16[16,4096]{1,0:T(8,128)(2,1)S(1)}, bf16[16,4096]{1,0:T(8,128)(2,1)}, u32[]{:S(2)}) copy-start(bf16[16,4096]{1,0:T(8,128)(2,1)} %get-tuple-element.11) | copy-start | bytes 393220

commit v3 on v2

--- a/solution.py
+++ b/solution.py
@@ -82,12 +82,12 @@
             device_id_type=MESH,
         )
 
-    def z_copy(j, step):
+    def z_copy(j, step, which):
         return pltpu.make_async_remote_copy(
-            src_ref=z_out.at[j, step - 1],
-            dst_ref=z_in.at[j, step - 1],
-            send_sem=z_send.at[j, step - 1],
-            recv_sem=z_recv.at[j, step - 1],
+            src_ref=z_out.at[j, step - 1, which],
+            dst_ref=z_in.at[j, step - 1, which],
+            send_sem=z_send.at[j, step - 1, which],
+            recv_sem=z_recv.at[j, step - 1, which],
             device_id=outer_peer(step),
             device_id_type=MESH,
         )
@@ -114,20 +114,28 @@
         qo_copy(0, which).start()
     pl.semaphore_wait(barrier, len(peers))
 
-    def start_inputs(j, carry):
+    def send_inputs(j):
         for step in head_steps:
             for which in range(2):
                 kv_copy(j, step, which).start()
 
-        @pl.when(j > 0)
-        def _():
+    def inputs_sent(j):
+        for step in head_steps:
             for which in range(2):
-                kv_local(j, which).start()
-                qo_copy(j, which).start()
-
+                kv_copy(j, step, which).wait_send()
+
+    send_inputs(0)
+
+    def start_local(j, carry):
+        for which in range(2):
+            kv_local(j, which).start()
+            qo_copy(j, which).start()
         return carry
 
-    lax.fori_loop(0, heads, start_inputs, 0)
+    lax.fori_loop(1, heads, start_local, 0)
+    inputs_sent(0)
+    if heads > 1:
+        send_inputs(1)
 
     def work(j):
         for which in range(2):
@@ -177,21 +185,28 @@
             part[j, which] = keep[j, which, :, 1 - me_lo].astype(BF16)
             x_copy(j, which).start()
 
+        @pl.when(j + 1 < heads)
+        def _():
+            inputs_sent(j + 1)
+
+        @pl.when(j + 2 < heads)
+        def _():
+            send_inputs(j + 2)
+
     def pair_sum(j):
-        for which in range(2):
+        for which in (1, 0):
             x_copy(j, which).wait()
             for step in range(1, outer):
                 hi = lax.rem(me_hi + step, outer)
                 total = keep[j, which, hi, me_lo] + x_in[j, which, hi].astype(F32)
                 z_out[j, step - 1, which] = total.astype(BF16)
+                z_copy(j, step, which).start()
             keep[j, which, me_hi, me_lo] += x_in[j, which, me_hi].astype(F32)
-        for step in range(1, outer):
-            z_copy(j, step).start()
 
     def outer_sum(j):
-        for step in range(1, outer):
-            z_copy(j, step).wait()
-        for which in range(2):
+        for which in (1, 0):
+            for step in range(1, outer):
+                z_copy(j, step, which).wait()
             total = keep[j, which, me_hi, me_lo]
             for step in range(1, outer):
                 total = total + z_in[j, step - 1, which].astype(F32)
@@ -223,7 +238,6 @@
         for which in range(2):
             out_copy(j, which).wait()
             for step in head_steps:
-                kv_copy(j, step, which).wait_send()
                 h_copy(j, step, which).wait()
         return carry
 
@@ -251,7 +265,7 @@
     return tuple(pl.pallas_call(
         functools.partial(kernel, sizes),
         out_shape=(big, big, small, small),
-        in_specs=[anywhere] * 4,
+        in_specs=[pl.BlockSpec(memory_space=pltpu.HBM)] * 4,
         out_specs=(anywhere, anywhere, vmem, vmem),
         scratch_shapes=[
             pltpu.VMEM((heads, rows, HEAD_DIM), BF16),
@@ -277,13 +291,13 @@
             dma((heads, 2)),
             dma((heads, 2)),
             dma((heads, 2)),
-            dma((heads, outer - 1)),
-            dma((heads, outer - 1)),
+            dma((heads, outer - 1, 2)),
+            dma((heads, outer - 1, 2)),
             dma((heads, head_group - 1, 2)),
             dma((heads, head_group - 1, 2)),
         ],
         compiler_params=pltpu.CompilerParams(
-            collective_id=0, has_side_effects=True, vmem_limit_bytes=56 * 1024 * 1024
+            collective_id=0, has_side_effects=True, vmem_limit_bytes=46 * 1024 * 1024
         ),
         cost_estimate=pl.CostEstimate(
             flops=flops,

time: 58.3 us -> 57.7 us (0.990)
  Pallas kernels: 51.7 us -> 50.4 us
    pallas_call x1, Pallas kernels: 51.7 us -> 50.4 us  [per_device(): pl.pallas_call(functools.partial(kernel, sizes), out_shape=(big, big, sma...]
    unnamed x10 -> x8, local copies, waits for them, and re-layouts: 5.87 us -> 6.39 us
where the time goes in v3:
time: 57.7 us; the launch traced here: 57.5 us
  Pallas kernels  50.4 us (87%)
  local copies, waits for them, and re-layouts  6.39 us (11%)
  between operations  0.65 us (1%)
    pallas_call x1, Pallas kernels, per_device(): pl.pallas_call(functools.partial(kernel, sizes), out_shape=(big, big, sma...  50.4 us
    unnamed x8, local copies, waits for them, and re-layouts  6.39 us

profile of v3, /device:TPU:0, one launch (start us, length us, event | category | flops | bytes accessed | tf_op | source)
XLA Modules:
  0.0 57.5 jit_solution(16614502652227026124)
XLA Ops:
  0.6 0.0 copy-start
  0.6 1.2 %copy-done = bf16[128,4096]{1,0:T(8,128)(2,1)S(1)} copy-done((bf16[128,4096]{1,0:T(8,128)(2,1)S(1)}, bf16[128,4096]{1,0:T(8,128)(2,1)}, u32[]{:S(2)}) %copy-start) | copy-done | bytes 1048600
  1.9 0.0 copy-start.1
  1.9 1.2 %copy-done.1 = bf16[128,4096]{1,0:T(8,128)(2,1)S(1)} copy-done((bf16[128,4096]{1,0:T(8,128)(2,1)S(1)}, bf16[128,4096]{1,0:T(8,128)(2,1)}, u32[]{:S(2)}) %copy-start.1) | copy-done | bytes 1048600
  3.1 50.4 %shard_map.75 = (bf16[1024,1024]{1,0:T(8,128)(2,1)S(1)}, bf16[1024,1024]{1,0:T(8,128)(2,1)S(1)}, bf16[16,4096]{1,0:T(8,128)(2,1)S(1)}, bf16[16,4096]{1,0:T(8,128)(2,1)S(1)}) custom-call(bf16[1024,1024]{1,0:T(8,128)(2,1)} %q_hbm.1, bf16[128,4096]{1,0:T(8,128)(2,1)S(1)} %copy-done, bf16[128,4096]{1,0:T(8,128)(2,1)S(1)} %copy-done.1, bf16[1024,1024]{1,0:T(8,128)(2,1)} %o_hbm.1), custom_call_target="tpu_custom_call" | custom-call | flops 6442450944 | bytes 10485760 | tf_op jit(solution)/shard_map/pallas_call | solution.py:265
  53.5 1.3 %copy.12 = bf16[1024,1024]{1,0:T(8,128)(2,1)} copy(bf16[1024,1024]{1,0:T(8,128)(2,1)S(1)} %get-tuple-element.8) | data formatting | bytes 4194304
  54.8 1.3 %copy.13 = bf16[1024,1024]{1,0:T(8,128)(2,1)} copy(bf16[1024,1024]{1,0:T(8,128)(2,1)S(1)} %get-tuple-element.9) | data formatting | bytes 4194304
  56.1 0.7 %copy.14 = bf16[16,4096]{1,0:T(8,128)(2,1)} copy(bf16[16,4096]{1,0:T(8,128)(2,1)S(1)} %get-tuple-element.10) | data formatting | bytes 262144
  56.8 0.7 %copy.15 = bf16[16,4096]{1,0:T(8,128)(2,1)} copy(bf16[16,4096]{1,0:T(8,128)(2,1)S(1)} %get-tuple-element.11) | data formatting | bytes 262144
Async XLA Ops:
  0.6 1.2 %copy-start = (bf16[128,4096]{1,0:T(8,128)(2,1)S(1)}, bf16[128,4096]{1,0:T(8,128)(2,1)}, u32[]{:S(2)}) copy-start(bf16[128,4096]{1,0:T(8,128)(2,1)} %k_hbm.1) | copy-start | bytes 3145732
  1.9 1.2 %copy-start.1 = (bf16[128,4096]{1,0:T(8,128)(2,1)S(1)}, bf16[128,4096]{1,0:T(8,128)(2,1)}, u32[]{:S(2)}) copy-start(bf16[128,4096]{1,0:T(8,128)(2,1)} %v_hbm.1) | copy-start | bytes 3145732

commit v4 on v3

--- a/solution.py
+++ b/solution.py
@@ -21,7 +21,7 @@
     att_hbm, dq_hbm, gk_ref, gv_ref,
     q_v, o_v, k_v, v_v, kt_v, vt_v, p_v, ds_v, att_v, dq_v,
     part, keep, x_in, z_out, z_in, h_out,
-    kv_send, kv_recv, kv_own, qo_sem, out_sem,
+    kv_send, kv_recv, forward_send, kv_own, qo_sem, out_sem,
     x_send, x_recv, z_send, z_recv, h_send, h_recv,
 ):
     heads, head_group, outer, rows, mem_rows, share, block = sizes
@@ -37,10 +37,14 @@
     def pair_peer():
         return me_hi * 2 + 1 - me_lo, me_h
 
+    def near_peer():
+        return (me_hi + 1 - 2 * parity) * 2 + me_lo, me_h
+
     def outer_peer(step):
         return lax.rem(me_hi + step, outer) * 2 + me_lo, me_h
 
-    head_steps = [s for s in range(2, head_group)] + [1]
+    head_steps = range(1, head_group)
+    parity = me_hi % 2
 
     def kv_copy(j, step, which):
         src, dst = ((k_hbm, k_v), (v_hbm, v_v))[which]
@@ -53,6 +57,27 @@
             send_sem=kv_send.at[j, step - 1, which],
             recv_sem=kv_recv.at[j, step - 1, which],
             device_id=peer,
+            device_id_type=MESH,
+        )
+
+    def sends(step):
+        same = head_peer(step)[1] // 2 == me_h // 2
+        return jnp.logical_or(same, me_h % 2 == parity)
+
+    def forwards(step):
+        source = lax.rem(me_h + head_group - step, head_group)
+        return jnp.logical_and(source // 2 != me_h // 2, source % 2 == parity)
+
+    def kv_forward(j, step, which):
+        source = lax.rem(me_h + head_group - step, head_group)
+        block_rows = pl.ds(pl.multiple_of(source * mem_rows, mem_rows), mem_rows)
+        buffer = (k_v, v_v)[which].at[j, block_rows, :]
+        return pltpu.make_async_remote_copy(
+            src_ref=buffer,
+            dst_ref=buffer,
+            send_sem=forward_send.at[j, step - 1, which],
+            recv_sem=kv_recv.at[j, step - 1, which],
+            device_id=near_peer(),
             device_id_type=MESH,
         )
 
@@ -116,13 +141,48 @@
 
     def send_inputs(j):
         for step in head_steps:
-            for which in range(2):
-                kv_copy(j, step, which).start()
+            @pl.when(sends(step))
+            def _():
+                for which in range(2):
+                    kv_copy(j, step, which).start()
 
     def inputs_sent(j):
         for step in head_steps:
-            for which in range(2):
-                kv_copy(j, step, which).wait_send()
+            @pl.when(sends(step))
+            def _():
+                for which in range(2):
+                    kv_copy(j, step, which).wait_send()
+
+    def forward_inputs(j):
+        for step in head_steps:
+            @pl.when(forwards(step))
+            def _():
+                for which in range(2):
+                    kv_copy(j, step, which).wait_recv()
+                    kv_forward(j, step, which).start()
+
+    def inputs_here(j):
+        for step in head_steps:
+            @pl.when(jnp.logical_not(forwards(step)))
+            def _():
+                for which in range(2):
+                    kv_copy(j, step, which).wait_recv()
+
+    def forwards_sent(j):
+        for step in head_steps:
+            @pl.when(forwards(step))
+            def _():
+                for which in range(2):
+                    kv_forward(j, step, which).wait_send()
+
+    def advance(j):
+        inputs_sent(j)
+
+        @pl.when(j + 1 < heads)
+        def _():
+            send_inputs(j + 1)
+
+        forward_inputs(j)
 
     send_inputs(0)
 
@@ -133,16 +193,23 @@
         return carry
 
     lax.fori_loop(1, heads, start_local, 0)
-    inputs_sent(0)
-    if heads > 1:
-        send_inputs(1)
+    advance(0)
+
+    def pair_sum(j):
+        for which in (1, 0):
+            x_copy(j, which).wait()
+            for step in range(1, outer):
+                hi = lax.rem(me_hi + step, outer)
+                total = keep[j, which, hi, me_lo] + x_in[j, which, hi].astype(F32)
+                z_out[j, step - 1, which] = total.astype(BF16)
+                z_copy(j, step, which).start()
+            keep[j, which, me_hi, me_lo] += x_in[j, which, me_hi].astype(F32)
 
     def work(j):
         for which in range(2):
             kv_local(j, which).wait()
             qo_copy(j, which).wait()
-            for step in head_steps:
-                kv_copy(j, step, which).wait_recv()
+        inputs_here(j)
         kt_v[...] = k_v[j].T
         vt_v[...] = v_v[j].T
 
@@ -158,6 +225,11 @@
             scores, dprobs = ahead
             if r + 1 < blocks:
                 ahead = products(r + 1)
+            if r == 1:
+                @pl.when(j + 1 < heads)
+                def _():
+                    advance(j + 1)
+
             at = slice(r * block, (r + 1) * block)
             top = jnp.max(scores, axis=0, keepdims=True)
             weights = jnp.exp2((scores - top) * (scale * math.log2(math.e)))
@@ -169,7 +241,7 @@
             ds_v[:, at] = dscores
             att = jnp.dot(vt_v[...], probs, preferred_element_type=F32).astype(BF16)
             att_v[j, at, :] = att.T
-            dq = (jnp.dot(kt_v[...], dscores, preferred_element_type=F32) * scale).astype(BF16)
+            dq = jnp.dot(kt_v[...], dscores, preferred_element_type=F32).astype(BF16)
             dq_v[j, at, :] = dq.T
 
         for which in range(2):
@@ -184,24 +256,10 @@
             keep[j, which] = total.reshape(outer, 2, piece, HEAD_DIM)
             part[j, which] = keep[j, which, :, 1 - me_lo].astype(BF16)
             x_copy(j, which).start()
-
-        @pl.when(j + 1 < heads)
-        def _():
-            inputs_sent(j + 1)
-
-        @pl.when(j + 2 < heads)
-        def _():
-            send_inputs(j + 2)
-
-    def pair_sum(j):
-        for which in (1, 0):
-            x_copy(j, which).wait()
-            for step in range(1, outer):
-                hi = lax.rem(me_hi + step, outer)
-                total = keep[j, which, hi, me_lo] + x_in[j, which, hi].astype(F32)
-                z_out[j, step - 1, which] = total.astype(BF16)
-                z_copy(j, step, which).start()
-            keep[j, which, me_hi, me_lo] += x_in[j, which, me_hi].astype(F32)
+            if which == 1:
+                @pl.when(j > 0)
+                def _():
+                    pair_sum(j - 1)
 
     def outer_sum(j):
         for which in (1, 0):
@@ -222,7 +280,7 @@
         def _():
             work(t)
 
-        @pl.when(jnp.logical_and(t >= 1, t <= heads))
+        @pl.when(t == heads)
         def _():
             pair_sum(t - 1)
 
@@ -235,6 +293,7 @@
     lax.fori_loop(0, heads + 2, turn, 0)
 
     def finish(j, carry):
+        forwards_sent(j)
         for which in range(2):
             out_copy(j, which).wait()
             for step in head_steps:
@@ -262,7 +321,7 @@
     anywhere = pl.BlockSpec(memory_space=pl.ANY)
     vmem = pl.BlockSpec(memory_space=pltpu.VMEM)
     dma = pltpu.SemaphoreType.DMA
-    return tuple(pl.pallas_call(
+    attended, dq, grad_keys, grad_values = pl.pallas_call(
         functools.partial(kernel, sizes),
         out_shape=(big, big, small, small),
         in_specs=[pl.BlockSpec(memory_space=pltpu.HBM)] * 4,
@@ -286,6 +345,7 @@
             pltpu.VMEM((heads, 2, head_group, share, HEAD_DIM), BF16),
             dma((heads, head_group - 1, 2)),
             dma((heads, head_group - 1, 2)),
+            dma((heads, head_group - 1, 2)),
             dma((heads, 2)),
             dma((heads, 2)),
             dma((heads, 2)),
@@ -297,14 +357,15 @@
             dma((heads, head_group - 1, 2)),
         ],
         compiler_params=pltpu.CompilerParams(
-            collective_id=0, has_side_effects=True, vmem_limit_bytes=46 * 1024 * 1024
+            collective_id=0, has_side_effects=True, vmem_limit_bytes=56 * 1024 * 1024
         ),
         cost_estimate=pl.CostEstimate(
             flops=flops,
             bytes_accessed=8 * rows * local_width + 4 * mem_rows * full_width,
             transcendentals=rows * memory * heads,
         ),
-    )(queries, mem_keys, mem_values, grad_out))
+    )(queries, mem_keys, mem_values, grad_out)
+    return attended, dq * jnp.bfloat16(HEAD_DIM ** -0.5), grad_keys, grad_values
 
 
 def solution(mesh):

time: 57.7 us -> 59.1 us (1.024)
  local copies, waits for them, and re-layouts: 6.39 us -> 2.64 us
  other arithmetic: 0 us -> 3.24 us
  Pallas kernels: 50.4 us -> 52.5 us
    unnamed x8 -> x9, local copies, waits for them, and re-layouts: 6.39 us -> 2.64 us
    mul x0 -> x1, other arithmetic: none -> 3.24 us  [per_device(): dq * jnp.bfloat16(HEAD_DIM ** (-0.5))]
    pallas_call x1, Pallas kernels: 50.4 us -> 52.5 us  [per_device(): pl.pallas_call(functools.partial(kernel, sizes), out_shape=(big, big, sma...]
where the time goes in v4:
time: 59.1 us; the launch traced here: 59 us
  Pallas kernels  52.5 us (89%)
  other arithmetic  3.24 us (5%)
  local copies, waits for them, and re-layouts  2.64 us (4%)
  between operations  0.65 us (1%)
    pallas_call x1, Pallas kernels, per_device(): pl.pallas_call(functools.partial(kernel, sizes), out_shape=(big, big, sma...  52.5 us
    mul x1, other arithmetic, per_device(): dq * jnp.bfloat16(HEAD_DIM ** (-0.5))  3.24 us
    unnamed x9, local copies, waits for them, and re-layouts  2.64 us

profile of v4, /device:TPU:0, one launch (start us, length us, event | category | flops | bytes accessed | tf_op | source)
XLA Modules:
  0.0 59.0 jit_solution(3922722445384899835)
XLA Ops:
  0.6 52.5 %shard_map.75 = (bf16[1024,1024]{1,0:T(8,128)(2,1)}, bf16[1024,1024]{1,0:T(8,128)(2,1)}, bf16[16,4096]{1,0:T(8,128)(2,1)}, bf16[16,4096]{1,0:T(8,128)(2,1)}) custom-call(bf16[1024,1024]{1,0:T(8,128)(2,1)} %q_hbm.1, bf16[128,4096]{1,0:T(8,128)(2,1)} %k_hbm.1, bf16[128,4096]{1,0:T(8,128)(2,1)} %v_hbm.1, bf16[1024,1024]{1,0:T(8,128)(2,1)} %o_hbm.1), custom_call_target="tpu_custom_call" | custom-call | flops 6442450944 | bytes 10485760 | tf_op jit(solution)/shard_map/pallas_call | solution.py:324
  53.1 0.0 copy-start
  53.1 3.2 %broadcast_multiply_fusion = bf16[1024,1024]{1,0:T(8,128)(2,1)} fusion(bf16[1024,1024]{1,0:T(8,128)(2,1)} %get-tuple-element.9), kind=kLoop, calls=%fused_computation | loop fusion | flops 1048576 | bytes 4194304 | tf_op jit(solution)/shard_map/mul | solution.py:368
  56.3 0.0 copy-done
  56.4 0.0 copy-start.2
  56.4 0.0 copy-start.1
  56.4 1.3 %copy.11 = bf16[1024,1024]{1,0:T(8,128)(2,1)} copy(bf16[1024,1024]{1,0:T(8,128)(2,1)S(1)} %copy-done) | data formatting | bytes 4194304
  57.7 0.0 copy-done.2
  57.7 0.7 %copy.12 = bf16[16,4096]{1,0:T(8,128)(2,1)} copy(bf16[16,4096]{1,0:T(8,128)(2,1)S(1)} %copy-done.2) | data formatting | bytes 262144
  58.3 0.0 copy-done.1
  58.3 0.7 %copy.13 = bf16[16,4096]{1,0:T(8,128)(2,1)} copy(bf16[16,4096]{1,0:T(8,128)(2,1)S(1)} %copy-done.1) | data formatting | bytes 262144
Async XLA Ops:
  53.1 3.3 %copy-start = (bf16[1024,1024]{1,0:T(8,128)(2,1)S(1)}, bf16[1024,1024]{1,0:T(8,128)(2,1)}, u32[]{:S(2)}) copy-start(bf16[1024,1024]{1,0:T(8,128)(2,1)} %get-tuple-element.16) | copy-start | bytes 6291460
  56.4 1.3 %copy-start.2 = (bf16[16,4096]{1,0:T(8,128)(2,1)S(1)}, bf16[16,4096]{1,0:T(8,128)(2,1)}, u32[]{:S(2)}) copy-start(bf16[16,4096]{1,0:T(8,128)(2,1)} %get-tuple-element.18) | copy-start | bytes 393220
  56.4 2.0 %copy-start.1 = (bf16[16,4096]{1,0:T(8,128)(2,1)S(1)}, bf16[16,4096]{1,0:T(8,128)(2,1)}, u32[]{:S(2)}) copy-start(bf16[16,4096]{1,0:T(8,128)(2,1)} %get-tuple-element.19) | copy-start | bytes 393220

commit v5 on v3

--- a/solution.py
+++ b/solution.py
@@ -104,6 +104,10 @@
             device_id_type=MESH,
         )
 
+    def over_memory(reduce, array):
+        groups = array.reshape(memory // 64, 64, block)
+        return reduce(reduce(groups, axis=0), axis=0, keepdims=True)
+
     barrier = pltpu.get_barrier_semaphore()
     peers = [head_peer(s) for s in range(1, head_group)]
     peers += [pair_peer()] + [outer_peer(s) for s in range(1, outer)]
@@ -159,13 +163,12 @@
             if r + 1 < blocks:
                 ahead = products(r + 1)
             at = slice(r * block, (r + 1) * block)
-            top = jnp.max(scores, axis=0, keepdims=True)
+            top = over_memory(jnp.max, scores)
             weights = jnp.exp2((scores - top) * (scale * math.log2(math.e)))
-            probs = (weights * (1.0 / jnp.sum(weights, axis=0, keepdims=True))).astype(BF16)
+            probs = (weights * (1.0 / over_memory(jnp.sum, weights))).astype(BF16)
             p_v[:, at] = probs
-            probs32 = probs.astype(F32)
-            delta = jnp.sum(probs32 * dprobs, axis=0, keepdims=True)
-            dscores = (probs32 * (dprobs - delta)).astype(BF16)
+            delta = over_memory(jnp.sum, probs.astype(F32) * dprobs)
+            dscores = probs * (dprobs - delta).astype(BF16)
             ds_v[:, at] = dscores
             att = jnp.dot(vt_v[...], probs, preferred_element_type=F32).astype(BF16)
             att_v[j, at, :] = att.T
@@ -297,7 +300,7 @@
             dma((heads, head_group - 1, 2)),
         ],
         compiler_params=pltpu.CompilerParams(
-            collective_id=0, has_side_effects=True, vmem_limit_bytes=46 * 1024 * 1024
+            collective_id=0, has_side_effects=True, vmem_limit_bytes=56 * 1024 * 1024
         ),
         cost_estimate=pl.CostEstimate(
             flops=flops,

time: 57.7 us -> 58 us (level)
  Pallas kernels: 50.4 us -> 51.3 us
    pallas_call x1, Pallas kernels: 50.4 us -> 51.3 us  [per_device(): pl.pallas_call(functools.partial(kernel, sizes), out_shape=(big, big, sma...]
    unnamed x8 -> x10, local copies, waits for them, and re-layouts: 6.39 us -> 5.87 us
where the time goes in v5:
time: 58 us; the launch traced here: 57.8 us
  Pallas kernels  51.3 us (88%)
  local copies, waits for them, and re-layouts  5.87 us (10%)
  between operations  0.65 us (1%)
    pallas_call x1, Pallas kernels, per_device(): pl.pallas_call(functools.partial(kernel, sizes), out_shape=(big, big, sma...  51.3 us
    unnamed x10, local copies, waits for them, and re-layouts  5.87 us

profile of v5, /device:TPU:0, one launch (start us, length us, event | category | flops | bytes accessed | tf_op | source)
XLA Modules:
  0.0 57.8 jit_solution(5823925836662063324)
XLA Ops:
  0.6 51.3 %shard_map.75 = (bf16[1024,1024]{1,0:T(8,128)(2,1)}, bf16[1024,1024]{1,0:T(8,128)(2,1)}, bf16[16,4096]{1,0:T(8,128)(2,1)}, bf16[16,4096]{1,0:T(8,128)(2,1)}) custom-call(bf16[1024,1024]{1,0:T(8,128)(2,1)} %q_hbm.1, bf16[128,4096]{1,0:T(8,128)(2,1)} %k_hbm.1, bf16[128,4096]{1,0:T(8,128)(2,1)} %v_hbm.1, bf16[1024,1024]{1,0:T(8,128)(2,1)} %o_hbm.1), custom_call_target="tpu_custom_call" | custom-call | flops 6442450944 | bytes 10485760 | tf_op jit(solution)/shard_map/pallas_call | solution.py:268
  51.9 0.0 copy-start
  51.9 3.2 %copy.12 = bf16[1024,1024]{1,0:T(8,128)(2,1)} copy(bf16[1024,1024]{1,0:T(8,128)(2,1)} %get-tuple-element.8) | data formatting | bytes 4194304
  55.2 0.0 copy-done
  55.2 0.0 copy-start.2
  55.2 0.0 copy-start.1
  55.2 1.3 %copy.13 = bf16[1024,1024]{1,0:T(8,128)(2,1)} copy(bf16[1024,1024]{1,0:T(8,128)(2,1)S(1)} %copy-done) | data formatting | bytes 4194304
  56.5 0.0 copy-done.2
  56.5 0.7 %copy.14 = bf16[16,4096]{1,0:T(8,128)(2,1)} copy(bf16[16,4096]{1,0:T(8,128)(2,1)S(1)} %copy-done.2) | data formatting | bytes 262144
  57.2 0.0 copy-done.1
  57.2 0.7 %copy.15 = bf16[16,4096]{1,0:T(8,128)(2,1)} copy(bf16[16,4096]{1,0:T(8,128)(2,1)S(1)} %copy-done.1) | data formatting | bytes 262144
Async XLA Ops:
  51.9 3.2 %copy-start = (bf16[1024,1024]{1,0:T(8,128)(2,1)S(1)}, bf16[1024,1024]{1,0:T(8,128)(2,1)}, u32[]{:S(2)}) copy-start(bf16[1024,1024]{1,0:T(8,128)(2,1)} %get-tuple-element.9) | copy-start | bytes 6291460
  55.2 1.3 %copy-start.2 = (bf16[16,4096]{1,0:T(8,128)(2,1)S(1)}, bf16[16,4096]{1,0:T(8,128)(2,1)}, u32[]{:S(2)}) copy-start(bf16[16,4096]{1,0:T(8,128)(2,1)} %get-tuple-element.10) | copy-start | bytes 393220
  55.2 2.0 %copy-start.1 = (bf16[16,4096]{1,0:T(8,128)(2,1)S(1)}, bf16[16,4096]{1,0:T(8,128)(2,1)}, u32[]{:S(2)}) copy-start(bf16[16,4096]{1,0:T(8,128)(2,1)} %get-tuple-element.11) | copy-start | bytes 393220

commit v6 on v5

--- a/solution.py
+++ b/solution.py
@@ -20,15 +20,17 @@
     q_hbm, k_hbm, v_hbm, o_hbm,
     att_hbm, dq_hbm, gk_ref, gv_ref,
     q_v, o_v, k_v, v_v, kt_v, vt_v, p_v, ds_v, att_v, dq_v,
-    part, keep, x_in, z_out, z_in, h_out,
+    part, keep, x_in, near_out, near_in, z_out, z_in, h_out,
     kv_send, kv_recv, kv_own, qo_sem, out_sem,
-    x_send, x_recv, z_send, z_recv, h_send, h_recv,
+    x_send, x_recv, near_send, near_recv, z_send, z_recv, h_send, h_recv,
 ):
     heads, head_group, outer, rows, mem_rows, share, block = sizes
     memory = mem_rows * head_group
     piece = head_group * share
     me_q, me_h = lax.axis_index("query"), lax.axis_index("head")
     me_hi, me_lo = me_q // 2, me_q % 2
+    me_far, me_near = me_hi // 2, me_hi % 2
+    far = outer // 2
     scale = HEAD_DIM ** -0.5
 
     def head_peer(step):
@@ -37,8 +39,11 @@
     def pair_peer():
         return me_hi * 2 + 1 - me_lo, me_h
 
-    def outer_peer(step):
-        return lax.rem(me_hi + step, outer) * 2 + me_lo, me_h
+    def near_peer():
+        return (me_far * 2 + 1 - me_near) * 2 + me_lo, me_h
+
+    def far_peer(step):
+        return (lax.rem(me_far + step, far) * 2 + me_near) * 2 + me_lo, me_h
 
     head_steps = [s for s in range(2, head_group)] + [1]
 
@@ -82,13 +87,23 @@
             device_id_type=MESH,
         )
 
+    def near_copy(j, which):
+        return pltpu.make_async_remote_copy(
+            src_ref=near_out.at[j, which],
+            dst_ref=near_in.at[j, which],
+            send_sem=near_send.at[j, which],
+            recv_sem=near_recv.at[j, which],
+            device_id=near_peer(),
+            device_id_type=MESH,
+        )
+
     def z_copy(j, step, which):
         return pltpu.make_async_remote_copy(
             src_ref=z_out.at[j, step - 1, which],
             dst_ref=z_in.at[j, step - 1, which],
             send_sem=z_send.at[j, step - 1, which],
             recv_sem=z_recv.at[j, step - 1, which],
-            device_id=outer_peer(step),
+            device_id=far_peer(step),
             device_id_type=MESH,
         )
 
@@ -110,7 +125,7 @@
 
     barrier = pltpu.get_barrier_semaphore()
     peers = [head_peer(s) for s in range(1, head_group)]
-    peers += [pair_peer()] + [outer_peer(s) for s in range(1, outer)]
+    peers += [pair_peer(), near_peer()] + [far_peer(s) for s in range(1, far)]
     for peer in peers:
         pl.semaphore_signal(barrier, inc=1, device_id=peer, device_id_type=MESH)
     for which in range(2):
@@ -199,19 +214,31 @@
     def pair_sum(j):
         for which in (1, 0):
             x_copy(j, which).wait()
-            for step in range(1, outer):
-                hi = lax.rem(me_hi + step, outer)
+            for f in range(far):
+                hi = f * 2 + 1 - me_near
                 total = keep[j, which, hi, me_lo] + x_in[j, which, hi].astype(F32)
-                z_out[j, step - 1, which] = total.astype(BF16)
+                near_out[j, which, f] = total.astype(BF16)
+            near_copy(j, which).start()
+            for f in range(far):
+                hi = f * 2 + me_near
+                keep[j, which, hi, me_lo] += x_in[j, which, hi].astype(F32)
+
+    def near_sum(j):
+        for which in (1, 0):
+            near_copy(j, which).wait()
+            for step in range(1, far):
+                f = lax.rem(me_far + step, far)
+                total = keep[j, which, f * 2 + me_near, me_lo]
+                z_out[j, step - 1, which] = (total + near_in[j, which, f].astype(F32)).astype(BF16)
                 z_copy(j, step, which).start()
-            keep[j, which, me_hi, me_lo] += x_in[j, which, me_hi].astype(F32)
+            keep[j, which, me_hi, me_lo] += near_in[j, which, me_far].astype(F32)
 
     def outer_sum(j):
         for which in (1, 0):
-            for step in range(1, outer):
+            for step in range(1, far):
                 z_copy(j, step, which).wait()
             total = keep[j, which, me_hi, me_lo]
-            for step in range(1, outer):
+            for step in range(1, far):
                 total = total + z_in[j, step - 1, which].astype(F32)
             for h in range(head_group):
                 h_out[j, which, h] = total[h * share : (h + 1) * share].astype(BF16)
@@ -225,17 +252,14 @@
         def _():
             work(t)
 
-        @pl.when(jnp.logical_and(t >= 1, t <= heads))
-        def _():
-            pair_sum(t - 1)
-
-        @pl.when(t >= 2)
-        def _():
-            outer_sum(t - 2)
+        for lag, stage in ((1, pair_sum), (2, near_sum), (3, outer_sum)):
+            @pl.when(jnp.logical_and(t >= lag, t < heads + lag))
+            def _():
+                stage(t - lag)
 
         return carry
 
-    lax.fori_loop(0, heads + 2, turn, 0)
+    lax.fori_loop(0, heads + 3, turn, 0)
 
     def finish(j, carry):
         for which in range(2):
@@ -284,8 +308,10 @@
             pltpu.VMEM((heads, 2, outer, piece, HEAD_DIM), BF16),
             pltpu.VMEM((heads, 2, outer, 2, piece, HEAD_DIM), F32),
             pltpu.VMEM((heads, 2, outer, piece, HEAD_DIM), BF16),
-            pltpu.VMEM((heads, outer - 1, 2, piece, HEAD_DIM), BF16),
-            pltpu.VMEM((heads, outer - 1, 2, piece, HEAD_DIM), BF16),
+            pltpu.VMEM((heads, 2, outer // 2, piece, HEAD_DIM), BF16),
+            pltpu.VMEM((heads, 2, outer // 2, piece, HEAD_DIM), BF16),
+            pltpu.VMEM((heads, outer // 2 - 1, 2, piece, HEAD_DIM), BF16),
+            pltpu.VMEM((heads, outer // 2 - 1, 2, piece, HEAD_DIM), BF16),
             pltpu.VMEM((heads, 2, head_group, share, HEAD_DIM), BF16),
             dma((heads, head_group - 1, 2)),
             dma((heads, head_group - 1, 2)),
@@ -294,8 +320,10 @@
             dma((heads, 2)),
             dma((heads, 2)),
             dma((heads, 2)),
-            dma((heads, outer - 1, 2)),
-            dma((heads, outer - 1, 2)),
+            dma((heads, 2)),
+            dma((heads, 2)),
+            dma((heads, outer // 2 - 1, 2)),
+            dma((heads, outer // 2 - 1, 2)),
             dma((heads, head_group - 1, 2)),
             dma((heads, head_group - 1, 2)),
         ],

time: 58 us -> 58.8 us (1.014)
  Pallas kernels: 51.3 us -> 52.2 us
    pallas_call x1, Pallas kernels: 51.3 us -> 52.2 us  [per_device(): pl.pallas_call(functools.partial(kernel, sizes), out_shape=(big, big, sma...]
where the time goes in v6:
time: 58.8 us; the launch traced here: 58.7 us
  Pallas kernels  52.2 us (89%)
  local copies, waits for them, and re-layouts  5.87 us (10%)
  between operations  0.65 us (1%)
    pallas_call x1, Pallas kernels, per_device(): pl.pallas_call(functools.partial(kernel, sizes), out_shape=(big, big, sma...  52.2 us
    unnamed x10, local copies, waits for them, and re-layouts  5.87 us

profile of v6, /device:TPU:0, one launch (start us, length us, event | category | flops | bytes accessed | tf_op | source)
XLA Modules:
  0.0 58.7 jit_solution(6721358587959378163)
XLA Ops:
  0.6 52.2 %shard_map.75 = (bf16[1024,1024]{1,0:T(8,128)(2,1)}, bf16[1024,1024]{1,0:T(8,128)(2,1)}, bf16[16,4096]{1,0:T(8,128)(2,1)}, bf16[16,4096]{1,0:T(8,128)(2,1)}) custom-call(bf16[1024,1024]{1,0:T(8,128)(2,1)} %q_hbm.1, bf16[128,4096]{1,0:T(8,128)(2,1)} %k_hbm.1, bf16[128,4096]{1,0:T(8,128)(2,1)} %v_hbm.1, bf16[1024,1024]{1,0:T(8,128)(2,1)} %o_hbm.1), custom_call_target="tpu_custom_call" | custom-call | flops 6442450944 | bytes 10485760 | tf_op jit(solution)/shard_map/pallas_call | solution.py:292
  52.8 0.0 copy-start
  52.8 3.2 %copy.12 = bf16[1024,1024]{1,0:T(8,128)(2,1)} copy(bf16[1024,1024]{1,0:T(8,128)(2,1)} %get-tuple-element.8) | data formatting | bytes 4194304
  56.0 0.0 copy-done
  56.0 0.0 copy-start.2
  56.0 0.0 copy-start.1
  56.1 1.3 %copy.13 = bf16[1024,1024]{1,0:T(8,128)(2,1)} copy(bf16[1024,1024]{1,0:T(8,128)(2,1)S(1)} %copy-done) | data formatting | bytes 4194304
  57.4 0.0 copy-done.2
  57.4 0.7 %copy.14 = bf16[16,4096]{1,0:T(8,128)(2,1)} copy(bf16[16,4096]{1,0:T(8,128)(2,1)S(1)} %copy-done.2) | data formatting | bytes 262144
  58.0 0.0 copy-done.1
  58.0 0.7 %copy.15 = bf16[16,4096]{1,0:T(8,128)(2,1)} copy(bf16[16,4096]{1,0:T(8,128)(2,1)S(1)} %copy-done.1) | data formatting | bytes 262144
Async XLA Ops:
  52.8 3.2 %copy-start = (bf16[1024,1024]{1,0:T(8,128)(2,1)S(1)}, bf16[1024,1024]{1,0:T(8,128)(2,1)}, u32[]{:S(2)}) copy-start(bf16[1024,1024]{1,0:T(8,128)(2,1)} %get-tuple-element.9) | copy-start | bytes 6291460
  56.0 1.3 %copy-start.2 = (bf16[16,4096]{1,0:T(8,128)(2,1)S(1)}, bf16[16,4096]{1,0:T(8,128)(2,1)}, u32[]{:S(2)}) copy-start(bf16[16,4096]{1,0:T(8,128)(2,1)} %get-tuple-element.10) | copy-start | bytes 393220
  56.0 2.0 %copy-start.1 = (bf16[16,4096]{1,0:T(8,128)(2,1)S(1)}, bf16[16,4096]{1,0:T(8,128)(2,1)}, u32[]{:S(2)}) copy-start(bf16[16,4096]{1,0:T(8,128)(2,1)} %get-tuple-element.11) | copy-start | bytes 393220
